TPU v7x, 256 devices: a whole 4x4x8 slice. The times are simulated.
256 devices in a mesh: dp: 16 (over z, y_hi), pipe: 2 (over core), tensor: 8 (over y_lo, x).
Axes of the slice: x: 4, y: 4 (y_hi: 2, y_lo: 2; y = y_hi * 2 + y_lo), z: 8, core: 2. Of those that a mesh axis runs over, the one named last changes fastest.
Arguments:
- section_input: bfloat16 [4, 2048, 6144], P(None, 'dp', 'tensor'), may hold values from -80 to 80
- gain: float32 [2, 6144], P('pipe', 'tensor'), may hold values from 0.5 to 1.5
- weight: bfloat16 [2, 6144, 6144], P('pipe', 'tensor'), may hold values from -0.078125 to 0.078125
- old_factor: float32 [2, 8, 48, 128, 128], P('pipe', 'tensor', 'dp'), may hold values from -0.09 to 0.09
- slot_table: int32 [48], replicated, may hold values from -1 to 20, as said below
- capture: int32 [2, 4], P('pipe'), may hold values from 0 to 1, as said below
Outputs:
- section_out: bfloat16 [2, 4, 2048, 6144], P('pipe', None, 'dp', 'tensor')
- new_factor: float32 [2, 8, 48, 128, 128], P('pipe', 'tensor', 'dp')
Inputs may be any that keep to these rules, and one draw needn't show every extreme that they name: `slot_table`: each of the 21 block numbers stands in exactly one slot, every other slot holds -1; slots k * 3 to (k + 1) * 3 - 1 belong to owner k, and some owner has all 3 slots used. `capture`: every section captures on at least one micro-batch.
All inputs are finite; a program needn't handle non-finite values.
Results may differ from a plain program's by a relative error of at most 0.007.
Values may be sent and summed in bfloat16 or wider, within the bound.
No kernel may reach another device: no remote copies, remote signals or barrier semaphores. Data moves between devices by JAX's collectives and lax.ppermute only.
A program may use at most 128 MiB of HBM per device.

v0:
```python
import jax
import jax.numpy as jnp
import numpy as np
from jax import lax
from jax.sharding import PartitionSpec as P

epsilon = 1e-06
factor_decay = 0.9


def shifted(shard, axis, by):
    size = lax.axis_size(axis)
    pairs = [(i, i + by) for i in range(size) if 0 <= i + by < size]
    return lax.ppermute(shard, axis, pairs)


def upper_blocks(block_count):
    return np.array(
        [row * block_count + col for row in range(block_count) for col in range(row, block_count)],
        dtype=np.int32,
    )


def local(section_input, gain, weight, old_factor, slot_table, capture):
    section_id = lax.axis_index("pipe")
    section_count = lax.axis_size("pipe")
    shard_rank = lax.axis_index("tensor")
    owner_count = lax.axis_size("dp")
    micro_count, tok_rows, shard_width = section_input.shape
    weight_rows = weight[0]
    full_width = weight_rows.shape[1]
    block_size = old_factor.shape[-1]
    capacity = old_factor.shape[2]
    block_count = shard_width // block_size
    flat_table = upper_blocks(block_count)
    block_total = flat_table.shape[0]
    matches = slot_table[:, None] == jnp.arange(block_total, dtype=jnp.int32)[None, :]
    flat_slot = jnp.sum(jnp.where(matches, jnp.asarray(flat_table)[None, :], 0), axis=1)
    slot_live = (slot_table >= 0)[:, None, None]
    total_tokens = tok_rows * owner_count
    captured = capture[0].astype(jnp.float32)
    capture_total = jnp.sum(captured)
    gain_row = gain[0]
    outputs = jnp.zeros((micro_count, tok_rows, shard_width), jnp.bfloat16)
    factor_sum = jnp.zeros((capacity, block_size, block_size), jnp.float32)
    received = jnp.zeros((tok_rows, shard_width), jnp.bfloat16)
    tick_count = micro_count + section_count - 1
    for moment in range(tick_count):
        micro_id = moment - section_id
        is_live = jnp.logical_and(micro_id >= 0, micro_id < micro_count)
        first_input = section_input[min(moment, micro_count - 1)]
        current = jnp.where(section_id == 0, first_input, received)
        widened = current.astype(jnp.float32)
        square_sum = lax.psum(jnp.sum(widened * widened, axis=1), "tensor")
        normed = (
            widened * lax.rsqrt(square_sum / full_width + epsilon)[:, None] * gain_row
        ).astype(jnp.bfloat16)
        partial_value = jnp.dot(normed, weight_rows, preferred_element_type=jnp.float32)
        summed = lax.psum(partial_value.astype(jnp.bfloat16), "tensor").astype(jnp.float32)
        own_cols = lax.dynamic_slice_in_dim(summed, shard_rank * shard_width, shard_width, 1)
        result = (widened + own_cols).astype(jnp.bfloat16)
        micro_slot = jnp.clip(micro_id, 0, micro_count - 1)
        previous = lax.dynamic_index_in_dim(outputs, micro_slot, 0, keepdims=False)
        outputs = lax.dynamic_update_index_in_dim(
            outputs, jnp.where(is_live, result, previous), micro_slot, 0
        )
        chosen = lax.dynamic_index_in_dim(captured, micro_slot, 0, keepdims=False)
        weighting = jnp.where(is_live, chosen, 0.0) / (capture_total * total_tokens)
        gram_local = lax.dot_general(
            normed, normed, (((0,), (0,)), ((), ())), preferred_element_type=jnp.float32
        )
        blocks_gram_local = gram_local * weighting
        tiled = blocks_gram_local.reshape(
            block_count, block_size, block_count, block_size
        ).transpose(0, 2, 1, 3)
        tiled = tiled.reshape(block_count * block_count, block_size, block_size)
        factor_sum = factor_sum + lax.psum_scatter(
            jnp.where(slot_live, tiled[flat_slot], jnp.float32(0.0)).astype(jnp.bfloat16),
            "dp",
            scatter_dimension=0,
            tiled=True,
        ).astype(jnp.float32)
        if moment + 1 < tick_count:
            received = shifted(result, "pipe", 1)
    own_slots = lax.dynamic_slice_in_dim(slot_table, lax.axis_index("dp") * capacity, capacity)
    updated = factor_decay * old_factor[0, 0] + (1.0 - factor_decay) * factor_sum
    new_factor = jnp.where((own_slots >= 0)[:, None, None], updated, jnp.float32(0.0))
    return (outputs[None], new_factor[None, None])


def solution(mesh):
    placed = (
        P(None, "dp", "tensor"),
        P("pipe", "tensor"),
        P("pipe", "tensor", None),
        P("pipe", "tensor", "dp", None, None),
        P(),
        P("pipe", None),
    )
    return jax.shard_map(
        local,
        mesh=mesh,
        in_specs=placed,
        out_specs=(P("pipe", None, "dp", "tensor"), P("pipe", "tensor", "dp", None, None)),
        check_vma=False,
    )
```

profile of v0, /device:TPU:1, one launch (start us, length us, event | category | flops | bytes accessed | tf_op | source)
XLA Modules:
  0.0 1609.3 jit_solution(16219547683434628981)
XLA Ops:
  8.3 16.8 %psum.70 = f32[128]{0:T(128)S(1)} all-reduce(f32[128]{0:T(128)S(1)} %fusion.27), channel_id=1, replica_groups=mesh['dp'=16,'pipe'=2,'tensor'=8] {'tensor'}, use_global_device_ids=true, to_apply=%region_1.2 | all-reduce | flops 128 | bytes 1024 | tf_op jit(solution)/shard_map/psum | solution.py:54
  25.8 6.4 fusion.10
  32.3 84.3 %all-reduce.6.cloned.1.call-done = bf16[128,6144]{1,0:T(8,128)(2,1)} async-done(((bf16[128,6144]{1,0:T(8,128)(2,1)}), bf16[128,6144]{1,0:T(8,128)(2,1)}) %all-reduce.6.cloned.1.call-update) | async-done | bytes 1572880 | tf_op jit(solution)/shard_map/psum | solution.py:59
  117.7 1.3 collective-permute-start
  119.0 6.1 collective-permute-done
  125.2 14.1 psum.72
  139.3 6.3 fusion.13
  145.7 82.0 %all-reduce.8.cloned.1.call-done = bf16[128,6144]{1,0:T(8,128)(2,1)} async-done(((bf16[128,6144]{1,0:T(8,128)(2,1)}), bf16[128,6144]{1,0:T(8,128)(2,1)}) %all-reduce.8.cloned.1.call-update) | async-done | bytes 1572880 | tf_op jit(solution)/shard_map/psum | solution.py:59
  228.7 1.3 collective-permute-start.1
  230.0 6.1 collective-permute-done.1
  236.2 14.1 psum.74
  250.4 6.3 fusion.16
  256.8 82.1 %all-reduce.10.cloned.1.call-done = bf16[128,6144]{1,0:T(8,128)(2,1)} async-done(((bf16[128,6144]{1,0:T(8,128)(2,1)}), bf16[128,6144]{1,0:T(8,128)(2,1)}) %all-reduce.10.cloned.1.call-update) | async-done | bytes 1572880 | tf_op jit(solution)/shard_map/psum | solution.py:59
  339.9 1.3 collective-permute-start.2
  341.2 6.1 collective-permute-done.2
  347.4 14.1 psum.76
  361.6 6.3 fusion.19
  371.7 1.4 reshape.111
  377.7 72.3 %all-reduce.12.cloned.1.call-done = bf16[128,6144]{1,0:T(8,128)(2,1)} async-done(((bf16[128,6144]{1,0:T(8,128)(2,1)}), bf16[128,6144]{1,0:T(8,128)(2,1)}) %all-reduce.12.cloned.1.call-update) | async-done | bytes 1572880 | tf_op jit(solution)/shard_map/psum | solution.py:59
  451.2 1.3 collective-permute-start.3
  452.5 1.1 broadcast_compare_fusion
  453.6 4.9 collective-permute-done.3
  459.6 14.2 psum.78
  473.8 6.3 fusion.22
  481.1 1.6 convolution_multiply_fusion.3
  482.7 3.8 reshape.113
  486.5 1.7 copy.15
  488.1 1.9 gather_fusion.1
  490.1 1.6 convolution_multiply_fusion.2
  491.7 2.3 reshape.115
  494.0 1.7 copy.16
  495.7 2.0 gather_fusion.2
  497.7 1.6 convolution_multiply_fusion.1
  499.3 2.2 reshape.117
  501.5 1.7 copy.17
  503.2 2.0 gather_fusion.3
  505.3 1.6 convolution_multiply_fusion
  506.9 2.2 reshape.119
  509.1 1.7 copy.18
  510.8 2.0 gather_fusion.4
  512.8 5.9 select_convert_fusion.4
  521.7 40.6 %all-reduce.14.cloned.1.call-done = bf16[128,6144]{1,0:T(8,128)(2,1)} async-done(((bf16[128,6144]{1,0:T(8,128)(2,1)}), bf16[128,6144]{1,0:T(8,128)(2,1)}) %all-reduce.14.cloned.1.call-update) | async-done | bytes 1572880 | tf_op jit(solution)/shard_map/psum | solution.py:59
  563.3 207.2 %reduce-scatter.14.cloned.1.call-done = bf16[3,128,128]{2,1,0:T(8,128)(2,1)} async-done(((bf16[48,128,128]{2,1,0:T(8,128)(2,1)}), bf16[3,128,128]{2,1,0:T(8,128)(2,1)}) %reduce-scatter.14.cloned.1.call-update) | async-done | bytes 98320 | tf_op jit(solution)/shard_map/reduce_scatter | solution.py:77
  770.5 207.9 %reduce-scatter.12.cloned.1.call-done = bf16[3,128,128]{2,1,0:T(8,128)(2,1)} async-done(((bf16[48,128,128]{2,1,0:T(8,128)(2,1)}), bf16[3,128,128]{2,1,0:T(8,128)(2,1)}) %reduce-scatter.12.cloned.1.call-update) | async-done | bytes 98320 | tf_op jit(solution)/shard_map/reduce_scatter | solution.py:77
  978.4 207.3 %reduce-scatter.10.cloned.1.call-done = bf16[3,128,128]{2,1,0:T(8,128)(2,1)} async-done(((bf16[48,128,128]{2,1,0:T(8,128)(2,1)}), bf16[3,128,128]{2,1,0:T(8,128)(2,1)}) %reduce-scatter.10.cloned.1.call-update) | async-done | bytes 98320 | tf_op jit(solution)/shard_map/reduce_scatter | solution.py:77
  1185.6 207.9 %reduce-scatter.8.cloned.1.call-done = bf16[3,128,128]{2,1,0:T(8,128)(2,1)} async-done(((bf16[48,128,128]{2,1,0:T(8,128)(2,1)}), bf16[3,128,128]{2,1,0:T(8,128)(2,1)}) %reduce-scatter.8.cloned.1.call-update) | async-done | bytes 98320 | tf_op jit(solution)/shard_map/reduce_scatter | solution.py:77
  1393.5 207.1 %reduce-scatter.6.cloned.1.call-done = bf16[3,128,128]{2,1,0:T(8,128)(2,1)} async-done(((bf16[48,128,128]{2,1,0:T(8,128)(2,1)}), bf16[3,128,128]{2,1,0:T(8,128)(2,1)}) %reduce-scatter.6.cloned.1.call-update) | async-done | bytes 98320 | tf_op jit(solution)/shard_map/reduce_scatter | solution.py:77
  1600.6 1.8 fusion.52
  (85 shorter events, 17.0 us)
Async XLA Ops:
  7.2 109.4 %all-reduce.6.cloned.1.call-start = ((), (), s32[]{:S(2)}) async-start(), calls=%async_computation.5 | async-start | bytes 3145728 | tf_op jit(solution)/shard_map/psum | solution.py:59
  32.2 84.5 %copy-start = (bf16[4,128,768]{2,1,0:T(8,128)(2,1)S(1)}, bf16[4,128,768]{2,1,0:T(8,128)(2,1)}, u32[]{:S(2)}) copy-start(bf16[4,128,768]{2,1,0:T(8,128)(2,1)} %param.7) | copy-start | bytes 2359300
  32.2 195.5 %all-reduce.8.cloned.1.call-start = ((), (), s32[]{:S(2)}) async-start(), calls=%async_computation.6 | async-start | bytes 3145728 | tf_op jit(solution)/shard_map/psum | solution.py:59
  117.7 7.4 collective-permute-start
  125.2 102.5 %copy-start.1 = (bf16[128,768]{1,0:T(8,128)(2,1)}, bf16[128,768]{1,0:T(8,128)(2,1)S(1)}, u32[]{:S(2)}) copy-start(bf16[128,768]{1,0:T(8,128)(2,1)S(1)} %get-tuple-element.15) | copy-start | bytes 589828
  145.6 193.3 %all-reduce.10.cloned.1.call-start = ((), (), s32[]{:S(2)}) async-start(), calls=%async_computation.7 | async-start | bytes 3145728 | tf_op jit(solution)/shard_map/psum | solution.py:59
  228.7 7.4 collective-permute-start.1
  236.2 102.7 %copy-start.3 = (bf16[128,768]{1,0:T(8,128)(2,1)}, bf16[128,768]{1,0:T(8,128)(2,1)S(1)}, u32[]{:S(2)}) copy-start(bf16[128,768]{1,0:T(8,128)(2,1)S(1)} %get-tuple-element.11) | copy-start | bytes 589828
  256.7 193.4 %all-reduce.12.cloned.1.call-start = ((), (), s32[]{:S(2)}) async-start(), calls=%async_computation.8 | async-start | bytes 3145728 | tf_op jit(solution)/shard_map/psum | solution.py:59
  339.9 7.4 collective-permute-start.2
  347.4 20.4 %copy-start.4 = (bf16[128,768]{1,0:T(8,128)(2,1)}, bf16[128,768]{1,0:T(8,128)(2,1)S(1)}, u32[]{:S(2)}) copy-start(bf16[128,768]{1,0:T(8,128)(2,1)S(1)} %get-tuple-element.7) | copy-start | bytes 589828
  361.6 6.3 copy-start.9
  367.8 0.7 copy-start.14
  367.9 194.4 %all-reduce.14.cloned.1.call-start = ((), (), s32[]{:S(2)}) async-start(), calls=%async_computation.9 | async-start | bytes 3145728 | tf_op jit(solution)/shard_map/psum | solution.py:59
  373.1 3.0 copy-start.15
  451.2 7.4 collective-permute-start.3
  459.6 14.2 copy-start.5
  473.8 6.3 copy-start.11
  480.1 0.9 copy-start.2
  480.2 290.3 %reduce-scatter.14.cloned.1.call-start = ((), (), s32[]{:S(2)}) async-start(), calls=%async_computation.14 | async-start | bytes 1671168 | tf_op jit(solution)/shard_map/reduce_scatter | solution.py:77
  495.7 2.0 copy-start.10
  503.2 2.0 copy-start.12
  510.8 2.0 copy-start.13
  518.8 459.6 %reduce-scatter.12.cloned.1.call-start = ((), (), s32[]{:S(2)}) async-start(), calls=%async_computation.13 | async-start | bytes 1671168 | tf_op jit(solution)/shard_map/reduce_scatter | solution.py:77
  519.5 666.1 %reduce-scatter.10.cloned.1.call-start = ((), (), s32[]{:S(2)}) async-start(), calls=%async_computation.12 | async-start | bytes 1671168 | tf_op jit(solution)/shard_map/reduce_scatter | solution.py:77
  520.3 873.2 %reduce-scatter.8.cloned.1.call-start = ((), (), s32[]{:S(2)}) async-start(), calls=%async_computation.11 | async-start | bytes 1671168 | tf_op jit(solution)/shard_map/reduce_scatter | solution.py:77
  520.3 1.3 copy-start.16
  521.0 1079.6 %reduce-scatter.6.cloned.1.call-start = ((), (), s32[]{:S(2)}) async-start(), calls=%async_computation.10 | async-start | bytes 1671168 | tf_op jit(solution)/shard_map/reduce_scatter | solution.py:77
  521.0 41.3 %copy-start.6 = (bf16[128,768]{1,0:T(8,128)(2,1)S(1)}, bf16[128,768]{1,0:T(8,128)(2,1)}, u32[]{:S(2)}) copy-start(bf16[128,768]{1,0:T(8,128)(2,1)} %copy-done.5) | copy-start | bytes 589828
  521.6 1079.0 %copy-start.8 = (f32[1,1,3,128,128]{4,3,2,1,0:T(8,128)S(1)}, f32[1,1,3,128,128]{4,3,2,1,0:T(8,128)}, u32[]{:S(2)}) copy-start(f32[1,1,3,128,128]{4,3,2,1,0:T(8,128)} %param.10) | copy-start | bytes 589828
  563.3 1039.1 %copy-start.7 = (bf16[1,4,128,768]{3,2,1,0:T(8,128)(2,1)}, bf16[1,4,128,768]{3,2,1,0:T(8,128)(2,1)S(1)}, u32[]{:S(2)}) copy-start(bf16[1,4,128,768]{3,2,1,0:T(8,128)(2,1)S(1)} %fusion.49) | copy-start | bytes 2359300
Sparse Core Ops, SparseCore 0:
  32.3 84.2 all-reduce.5
  145.7 81.9 all-reduce.7
  256.8 82.0 all-reduce.9
  368.0 82.0 all-reduce.11
  480.3 81.9 all-reduce.13
  566.0 204.4 reduce-scatter.13
  774.8 203.4 reduce-scatter.11
  982.2 203.3 reduce-scatter.9
  1190.0 203.4 reduce-scatter.7
  1397.2 203.3 reduce-scatter.5
where the time goes:
time: 1610 us
  waiting for transfers between devices  1420 us (88%)
  blocking collectives  73.3 us (5%)
  matrix products  38.6 us (2%)
  local copies, waits for them, and re-layouts  29.9 us (2%)
  other arithmetic  18.8 us (1%)
  between operations  18.5 us (1%)
    reduce_scatter x5, waiting for transfers between devices, local(): lax.psum_scatter(jnp.where(slot_live, tiled[flat_slot], jnp.float32(0.0))...  1040 us
    psum x5, waiting for transfers between devices, local(): lax.psum(partial_value.astype(jnp.bfloat16), 'tensor').astype(jnp.float32)  361 us
    psum x5, blocking collectives, local(): square_sum = lax.psum(jnp.sum(widened * widened, axis=1), 'tensor')  73.3 us
  transfers between devices with their start and end apart: 14, of which 14 were waited for; matrix products, arithmetic and copies ran while one was open for 3% of the time, Pallas kernels for 0%

commit v1 on v0

v1 whole, which is shorter than its diff:
```python
import jax
import jax.numpy as jnp
from jax import lax
from jax.experimental import pallas as pl
from jax.experimental.pallas import tpu as pltpu
from jax.sharding import PartitionSpec as P

EPS = 1e-06
DECAY = 0.9
BF = jnp.bfloat16
F32 = jnp.float32
NX, NYL, NZ, NYH = 4, 2, 8, 2
NT = NX * NYL
NDP = NZ * NYH
ROWS_A = 224
VMEM = 32 * 1024 * 1024


def tensor_perm(value, pipes, to):
    pairs = [(p * NT + t, p * NT + to(t)) for p in pipes for t in range(NT)]
    return lax.ppermute(value, ("pipe", "tensor"), pairs)


def x_by(k):
    return lambda t: (t // NX) * NX + (t % NX + k) % NX


def y_other(t):
    return t ^ NX


def core_perm(value, source):
    return lax.ppermute(value, "pipe", [(source, 1 - source)])


def dp_perm(value, pipe, pipe_to, to):
    pairs = [(d * 2 + pipe, to(d) * 2 + pipe_to) for d in range(NDP)]
    return lax.ppermute(value, ("dp", "pipe"), pairs)


def z_by(k):
    return lambda d: ((d // NYH + k) % NZ) * NYH + d % NYH


def project(rows, weight, ids, plan, shapes):
    count, (total, width) = len(plan), rows.shape
    half = total // 2

    def kernel(ids_ref, x_ref, w_ref, *outs):
        del ids_ref
        step = pl.program_id(0)
        y = jnp.dot(x_ref[...], w_ref[...], preferred_element_type=F32).astype(BF)
        for i, places in enumerate(plan):

            @pl.when(step == i)
            def _(places=places):
                for h, (o, at) in enumerate(places):
                    outs[o][at] = y[h * half : (h + 1) * half]

    out_shapes = [jax.ShapeDtypeStruct((n, half, width), BF) for n in shapes]
    return pl.pallas_call(
        kernel,
        grid_spec=pltpu.PrefetchScalarGridSpec(
            num_scalar_prefetch=1,
            grid=(count,),
            in_specs=[
                pl.BlockSpec((total, width), lambda i, ids: (0, 0)),
                pl.BlockSpec((width, width), lambda i, ids: (0, ids[i])),
            ],
            out_specs=[pl.BlockSpec(s.shape, lambda i, ids: (0, 0, 0)) for s in out_shapes],
        ),
        out_shape=out_shapes,
        compiler_params=pltpu.CompilerParams(
            dimension_semantics=("arbitrary",), vmem_limit_bytes=VMEM
        ),
        cost_estimate=pl.CostEstimate(
            flops=2 * total * width * width * count,
            bytes_accessed=2 * count * width * (width + total),
            transcendentals=0,
        ),
    )(ids, rows, weight)


def f32(v):
    return v.astype(F32)


def ring_reduce(pipe, first_p, first_m, next_p, next_m, own0, own1):
    n = first_p.shape[0] // 2
    got_p = tensor_perm(first_p, (pipe,), x_by(1))
    got_m = tensor_perm(first_m, (pipe,), x_by(-1))
    second_p = (f32(next_p) + f32(got_p[:n])).astype(BF)
    second_m = (f32(next_m) + f32(got_m[:n])).astype(BF)
    last_p = tensor_perm(second_p, (pipe,), x_by(1))
    last_m = tensor_perm(second_m, (pipe,), x_by(-1))
    h0 = f32(own0) + f32(got_m[n:]) + f32(last_p)
    h1 = f32(own1) + f32(got_p[n:]) + f32(last_m)
    return h0, h1


def reduce_projection(pipe, rows_a, rows_b, weight, t):
    yl, x = t // NX, t % NX
    ring = [(x + 2) % NX, (x + 1) % NX, (x + 3) % NX, x]
    mine = [yl * NX + r for r in ring]
    other = [(1 - yl) * NX + r for r in ring]
    width = rows_a.shape[1]
    plan_a = [((0, 0), (1, 0)), ((2, 0), (0, 1)), ((1, 1), (3, 0)), ((4, 0), (4, 1))]
    flat = [0, 2, 4, 5, 6]
    plan_y = [tuple((0, flat[o] + at) for o, at in places) for places in plan_a]
    (sent_y,) = project(rows_a, weight, jnp.stack(other), plan_y, [8])
    got_y = tensor_perm(sent_y, (pipe,), y_other)
    ids_b = [c for pair in zip(mine, other) for c in pair]
    plan_b = []
    for places in plan_a:
        for which in range(2):
            plan_b.append(tuple((o, 2 * at + which) for o, at in places))
    b_fp, b_fm, b_np, b_nm, b_own = project(
        rows_b, weight, jnp.stack(ids_b), plan_b, [4, 4, 2, 2, 4]
    )
    b0, b1 = ring_reduce(pipe, b_fp, b_fm, b_np, b_nm, b_own[:2], b_own[2:])
    a_fp, a_fm, a_np, a_nm, a_own = project(
        rows_a, weight, jnp.stack(mine), plan_a, [2, 2, 1, 1, 2]
    )
    add = lambda own, at: f32(own) + f32(got_y[at : at + own.shape[0]])
    a0, a1 = ring_reduce(
        pipe,
        add(a_fp, 0).astype(BF),
        add(a_fm, 2).astype(BF),
        add(a_np, 4),
        add(a_nm, 5),
        add(a_own[:1], 6),
        add(a_own[1:], 7),
    )
    away = jnp.concatenate([b0[1], b1[1]], axis=0).astype(BF)
    got_b = tensor_perm(away, (pipe,), y_other)
    sum_b = jnp.concatenate([b0[0], b1[0]], axis=0) + f32(got_b)
    sum_a = jnp.concatenate([a0[0], a1[0]], axis=0)
    return sum_a.reshape(-1, width), sum_b


def square_sum(rows, pipes):
    wide = f32(rows)
    total = jnp.sum(wide * wide, axis=-1).reshape(-1, 128)
    total = total + tensor_perm(total, pipes, y_other)
    total = total + tensor_perm(total, pipes, lambda t: t ^ 1)
    total = total + tensor_perm(total, pipes, lambda t: t ^ 2)
    return total


def gram_parts(normed, captured, z, blocks, block, total_tokens):
    micro = captured.shape[0]
    rows, width = normed.shape
    each = rows // micro
    sub = block // NZ
    count = blocks * (blocks + 1) // 2

    def kernel(cap_ref, z_ref, n_ref, *rest):
        outs, left, grams = rest[:NZ], rest[NZ], rest[NZ + 1]
        live = cap_ref[0]
        for m in range(1, micro):
            live = live + cap_ref[m]
        for m in range(micro):
            part = pl.ds(m * each, each)
            left[part] = (f32(n_ref[part]) * cap_ref[m]).astype(BF)
        scale = 1.0 / jnp.full((1, 1), live * total_tokens, F32)
        b = 0
        for i in range(blocks):
            g = lax.dot_general(
                left[:, i * block : (i + 1) * block],
                n_ref[:, i * block :],
                (((0,), (0,)), ((), ())),
                preferred_element_type=F32,
            )
            g = g * scale
            for j in range(blocks - i):
                grams[b] = g[:, j * block : (j + 1) * block]
                b += 1
        for k in range(NZ):
            at = pl.multiple_of(lax.rem(z_ref[0] + k, NZ) * sub, sub)
            outs[k][...] = grams[:, pl.ds(at, sub), :].astype(BF)

    smem = pl.BlockSpec(memory_space=pltpu.SMEM)
    vmem = pl.BlockSpec(memory_space=pltpu.VMEM)
    return pl.pallas_call(
        kernel,
        in_specs=[smem, smem, vmem],
        out_specs=[vmem] * NZ,
        out_shape=[jax.ShapeDtypeStruct((count, sub, block), BF)] * NZ,
        scratch_shapes=[
            pltpu.VMEM((rows, width), BF),
            pltpu.VMEM((count, block, block), F32),
        ],
        compiler_params=pltpu.CompilerParams(vmem_limit_bytes=VMEM),
        cost_estimate=pl.CostEstimate(
            flops=rows * width * width, bytes_accessed=2 * rows * width, transcendentals=0
        ),
    )(captured, z[None], normed)


def pick_slots(near, far, ids, capacity):
    _, sub, block = near.shape

    def kernel(ids_ref, near_ref, far_ref, *outs):
        for k in range(NZ):
            for i in range(capacity):
                at = ids_ref[k * capacity + i]
                outs[k][i] = (f32(near_ref[at]) + f32(far_ref[at])).astype(BF)

    smem = pl.BlockSpec(memory_space=pltpu.SMEM)
    vmem = pl.BlockSpec(memory_space=pltpu.VMEM)
    return pl.pallas_call(
        kernel,
        in_specs=[smem, vmem, vmem],
        out_specs=[vmem] * NZ,
        out_shape=[jax.ShapeDtypeStruct((capacity, sub, block), BF)] * NZ,
        compiler_params=pltpu.CompilerParams(vmem_limit_bytes=VMEM),
    )(ids, near, far)


def update_factor(old, live, z, parts0, parts1):
    capacity, block, _ = old.shape
    sub = block // NZ

    def kernel(live_ref, z_ref, old_ref, *rest):
        first, second, out = rest[:NZ], rest[NZ : 2 * NZ], rest[2 * NZ]
        for k in range(NZ):
            at = pl.multiple_of(lax.rem(z_ref[0] + NZ - k, NZ) * sub, sub)
            for i in range(capacity):
                got = f32(first[k][i]) + f32(second[k][i])
                new = DECAY * old_ref[i, pl.ds(at, sub), :] + (1.0 - DECAY) * got
                out[i, pl.ds(at, sub), :] = jnp.where(live_ref[i] > 0, new, 0.0)

    smem = pl.BlockSpec(memory_space=pltpu.SMEM)
    vmem = pl.BlockSpec(memory_space=pltpu.VMEM)
    return pl.pallas_call(
        kernel,
        in_specs=[smem, smem] + [vmem] * (1 + 2 * NZ),
        out_specs=vmem,
        out_shape=jax.ShapeDtypeStruct(old.shape, F32),
        compiler_params=pltpu.CompilerParams(vmem_limit_bytes=VMEM),
    )(live, z[None], old, *parts0, *parts1)


def factor_parts(pipe, rows, squares, gain, captured, slot_table, capacity, block):
    d = lax.axis_index("dp")
    z, yh = d // NYH, d % NYH
    width = rows.shape[1]
    full = width * NT
    scale = lax.rsqrt(squares / full + EPS).reshape(-1, 1)
    normed = (f32(rows) * scale * gain).astype(BF)
    tokens = rows.shape[0] // captured.shape[0] * NDP
    parts = gram_parts(normed, captured, z, width // block, block, float(tokens))
    total = f32(parts[0])
    for k in range(1, NZ):
        total = total + f32(dp_perm(parts[k], pipe, pipe, z_by(k)))
    near = total.astype(BF)
    far = dp_perm(near, pipe, pipe, lambda v: v ^ 1)
    table = jnp.maximum(slot_table, 0).reshape(NZ, NYH, capacity)
    table = lax.dynamic_index_in_dim(table, yh, 1, keepdims=False)
    ids = jnp.roll(table, -z, axis=0).reshape(-1)
    picked = pick_slots(near, far, ids, capacity)
    return [dp_perm(picked[k], pipe, 1 - pipe, z_by(k)) for k in range(NZ)]


def local(section_input, gain, weight, old_factor, slot_table, capture):
    pipe = lax.axis_index("pipe")
    t = lax.axis_index("tensor")
    d = lax.axis_index("dp")
    micro, each, width = section_input.shape
    w = weight[0]
    old = old_factor[0, 0]
    capacity, block, _ = old.shape
    x0 = section_input.reshape(micro * each, width)
    full = width * NT

    params = jnp.concatenate([gain[0], capture[0].astype(F32)])
    params = lax.ppermute(params, "pipe", [(0, 1), (1, 0)])
    gain_other, cap_other = params[:width], params[width:]

    def scaled(rows):
        return (f32(rows) * gain[0]).astype(BF)

    def finish(rows, squares, total):
        return (f32(rows) + total * lax.rsqrt(squares / full + EPS)[:, None]).astype(BF)

    squares0 = square_sum(x0, (0, 1))
    sum_a, sum_b = reduce_projection(0, scaled(x0[:ROWS_A]), scaled(x0[ROWS_A:]), w, t)
    flat0 = squares0.reshape(-1)
    x1a = finish(x0[:ROWS_A], flat0[:ROWS_A], sum_a)
    x1b = finish(x0[ROWS_A:], flat0[ROWS_A:], sum_b)
    parts0 = factor_parts(
        1, x0, squares0, gain_other, cap_other, slot_table, capacity, block
    )
    in_a, in_b = core_perm(x1a, 0), core_perm(x1b, 0)
    x1 = jnp.concatenate([x1a, x1b], axis=0)
    squares1 = square_sum(x1, (0,))
    in_squares = core_perm(squares1, 0).reshape(-1)
    sum_a, sum_b = reduce_projection(1, scaled(in_a), scaled(in_b), w, t)
    parts1 = factor_parts(
        0, x1, squares1, gain_other, cap_other, slot_table, capacity, block
    )
    x2 = jnp.concatenate(
        [
            finish(in_a, in_squares[:ROWS_A], sum_a),
            finish(in_b, in_squares[ROWS_A:], sum_b),
        ],
        axis=0,
    )
    out = jnp.where(pipe == 0, x1, x2).reshape(1, micro, each, width)
    own = lax.dynamic_slice_in_dim(slot_table, d * capacity, capacity)
    live = (own >= 0).astype(jnp.int32)
    new = update_factor(old, live, d // NYH, parts0, parts1)
    return (out, new[None, None])


def solution(mesh):
    placed = (
        P(None, "dp", "tensor"),
        P("pipe", "tensor"),
        P("pipe", "tensor", None),
        P("pipe", "tensor", "dp", None, None),
        P(),
        P("pipe", None),
    )
    return jax.shard_map(
        local,
        mesh=mesh,
        in_specs=placed,
        out_specs=(P("pipe", None, "dp", "tensor"), P("pipe", "tensor", "dp", None, None)),
        check_vma=False,
    )
```

time: 1610 us -> 344 us (0.21)
  waiting for transfers between devices: 1420 us -> 17.8 us
  starting transfers between devices: 5.75 us -> 265 us
  blocking collectives: 73.3 us -> 0 us
  matrix products: 38.6 us -> 0 us
  Pallas kernels: 0 us -> 30.1 us
  between operations: 18.5 us -> 2 us
    reduce_scatter x5 -> x0, waiting for transfers between devices: 1040 us -> none  [local(): lax.psum_scatter(jnp.where(slot_live, tiled[flat_slot], jnp.float32(0.0))...]
    psum x5 -> x0, waiting for transfers between devices: 361 us -> none  [local(): lax.psum(partial_value.astype(jnp.bfloat16), 'tensor').astype(jnp.float32)]
    ppermute x4 -> x62, starting transfers between devices: 5.17 us -> 265 us  [the longest x32 163 us: dp_perm(): return lax.ppermute(value, ('dp', 'pipe'), pairs)]
    psum x5 -> x0, blocking collectives: 73.3 us -> none  [local(): square_sum = lax.psum(jnp.sum(widened * widened, axis=1), 'tensor')]
    dot_general x10 -> x0, matrix products: 38.6 us -> none  [the longest x5 31.5 us: local(): jnp.dot(normed, weight_rows, preferred_element_type=jnp.float32)]
    pallas_call x0 -> x11, Pallas kernels: none -> 30.1 us  [the longest x6 24.4 us: project(): pl.pallas_call(kernel, grid_spec=pltpu.PrefetchScalarGridSpec(num_scalar_...]
  transfers between devices with their start and end apart: 14 -> 62, of which waited for: 14 -> 12; matrix products, arithmetic and copies ran while one was open for 3% -> 3% of each run, Pallas kernels for 0% -> 7%
where the time goes in v1:
time: 344 us; the launch traced here: 343 us
  starting transfers between devices  265 us (77%)
  Pallas kernels  30.1 us (9%)
  waiting for transfers between devices  17.8 us (5%)
  local copies, waits for them, and re-layouts  16.2 us (5%)
  other arithmetic  11.5 us (3%)
    ppermute x32, starting transfers between devices, dp_perm(): return lax.ppermute(value, ('dp', 'pipe'), pairs)  163 us
    ppermute x26, starting transfers between devices, tensor_perm(): return lax.ppermute(value, ('pipe', 'tensor'), pairs)  84.1 us
    pallas_call x6, Pallas kernels, project(): pl.pallas_call(kernel, grid_spec=pltpu.PrefetchScalarGridSpec(num_scalar_...  24.4 us
    unnamed x36, local copies, waits for them, and re-layouts  15.4 us
    ppermute x1, starting transfers between devices, local(): params = lax.ppermute(params, 'pipe', [(0, 1), (1, 0)])  14.3 us
    ppermute x32, waiting for transfers between devices, dp_perm(): return lax.ppermute(value, ('dp', 'pipe'), pairs)  7.82 us
    ppermute x26, waiting for transfers between devices, tensor_perm(): return lax.ppermute(value, ('pipe', 'tensor'), pairs)  7.54 us
  transfers between devices with their start and end apart: 62, of which 12 were waited for; matrix products, arithmetic and copies ran while one was open for 3% of the time, Pallas kernels for 7%

profile of v1, /device:TPU:1, one launch (start us, length us, event | category | flops | bytes accessed | tf_op | source)
XLA Modules:
  0.0 342.6 jit_solution(10627686467025060088)
XLA Ops:
  2.7 3.7 %copy-done = bf16[1,768,6144]{2,1,0:T(8,128)(2,1)S(1)} copy-done((bf16[1,768,6144]{2,1,0:T(8,128)(2,1)S(1)}, bf16[1,768,6144]{2,1,0:T(8,128)(2,1)}, u32[]{:S(2)}) %copy-start) | copy-done | bytes 9437208
  6.4 6.0 %shard_map.79 = (bf16[4,144,768]{2,1,0:T(8,128)(2,1)S(1)}, bf16[4,144,768]{2,1,0:T(8,128)(2,1)S(1)}, bf16[2,144,768]{2,1,0:T(8,128)(2,1)S(1)}, bf16[2,144,768]{2,1,0:T(8,128)(2,1)S(1)}, bf16[4,144,768]{2,1,0:T(8,128)(2,1)S(1)}) custom-call(s32[8]{0:T(128)S(1)} %stack.32.ids_ref, bf16[288,768]{1,0:T(8,128)(2,1)S(1)} %fusion.3.x_ref, ...), custom_call_target="tpu_custom_call" | custom-call | flops 2717908992 | bytes 12976128 | tf_op jit(solution)/shard_map/pallas_call | solution.py:61
  14.0 18.3 %collective-permute-start.5 = (f32[4,128]{1,0:T(4,128)S(1)}, f32[4,128]{1,0:T(4,128)S(1)}, u32[]{:S(2)}, u32[]{:S(2)}) collective-permute-start(f32[4,128]{1,0:T(4,128)S(1)} %multiply_reduce_fusion), channel_id=1, source_target_pairs={{0,4},{1,5},{2,6},{3,7},{4,0},{5,1},{6,2},{7,3},{8,12},{9,13},{10,... | collective-permute-start | bytes 6152 | tf_op jit(solution)/shard_map/ppermute | solution.py:21
  32.5 2.9 shard_map.78
  36.1 14.3 %collective-permute-start.29 = (f32[772]{0:T(1024)S(1)}, f32[772]{0:T(1024)S(1)}, u32[]{:S(2)}, u32[]{:S(2)}) collective-permute-start(f32[772]{0:T(1024)S(1)} %pad_maximum_fusion.3), channel_id=1, source_target_pairs={{0,8},{8,0},{1,9},{9,1},{2,10},{10,2},{3,11},{11,3},{4,12},{12,4},... | collective-permute-start | bytes 9272 | tf_op jit(solution)/shard_map/ppermute | solution.py:277
  50.5 11.8 %collective-permute-start.6 = (f32[4,128]{1,0:T(4,128)S(1)}, f32[4,128]{1,0:T(4,128)S(1)}, u32[]{:S(2)}, u32[]{:S(2)}) collective-permute-start(f32[4,128]{1,0:T(4,128)S(1)} %add.314), channel_id=1, source_target_pairs={{0,1},{1,0},{2,3},{3,2},{4,5},{5,4},{6,7},{7,6},{8,9},{9,8},{10,11... | collective-permute-start | bytes 6152 | tf_op jit(solution)/shard_map/ppermute | solution.py:21
  62.4 2.3 collective-permute-done.6
  64.7 12.2 %collective-permute-start.7 = (f32[4,128]{1,0:T(4,128)S(1)}, f32[4,128]{1,0:T(4,128)S(1)}, u32[]{:S(2)}, u32[]{:S(2)}) collective-permute-start(f32[4,128]{1,0:T(4,128)S(1)} %add.315), channel_id=1, source_target_pairs={{0,2},{1,3},{2,0},{3,1},{4,6},{5,7},{6,4},{7,5},{8,10},{9,11},{10,... | collective-permute-start | bytes 6152 | tf_op jit(solution)/shard_map/ppermute | solution.py:21
  76.9 2.9 shard_map.77
  91.7 2.0 shard_map.83
  93.7 59.3 %collective-permute-start.36 = (bf16[21,16,128]{2,1,0:T(8,128)(2,1)S(1)}, bf16[21,16,128]{2,1,0:T(8,128)(2,1)S(1)}, u32[]{:S(2)}, u32[]{:S(2)}) collective-permute-start(bf16[21,16,128]{2,1,0:T(8,128)(2,1)S(1)} %get-tuple-element.82), channel_id=1, source_target_pairs={{8,232},{24,248},{40,8},{56,24},{72,40},{88,56},{104,72},{120,88},... | collective-permute-start | bytes 258056 | tf_op jit(solution)/shard_map/ppermute | solution.py:38
  153.0 12.9 %collective-permute-start.35 = (bf16[21,16,128]{2,1,0:T(8,128)(2,1)S(1)}, bf16[21,16,128]{2,1,0:T(8,128)(2,1)S(1)}, u32[]{:S(2)}, u32[]{:S(2)}) collective-permute-start(bf16[21,16,128]{2,1,0:T(8,128)(2,1)S(1)} %get-tuple-element.81), channel_id=1, source_target_pairs={{8,200},{24,216},{40,232},{56,248},{72,8},{88,24},{104,40},{120,56... | collective-permute-start | bytes 258056 | tf_op jit(solution)/shard_map/ppermute | solution.py:38
  165.9 12.9 %collective-permute-start.34 = (bf16[21,16,128]{2,1,0:T(8,128)(2,1)S(1)}, bf16[21,16,128]{2,1,0:T(8,128)(2,1)S(1)}, u32[]{:S(2)}, u32[]{:S(2)}) collective-permute-start(bf16[21,16,128]{2,1,0:T(8,128)(2,1)S(1)} %get-tuple-element.80), channel_id=1, source_target_pairs={{8,168},{24,184},{40,200},{56,216},{72,232},{88,248},{104,8},{120,... | collective-permute-start | bytes 258056 | tf_op jit(solution)/shard_map/ppermute | solution.py:38
  178.8 8.1 %collective-permute-start.33 = (bf16[21,16,128]{2,1,0:T(8,128)(2,1)}, bf16[21,16,128]{2,1,0:T(8,128)(2,1)}, u32[]{:S(2)}, u32[]{:S(2)}) collective-permute-start(bf16[21,16,128]{2,1,0:T(8,128)(2,1)} %get-tuple-element.79), channel_id=1, source_target_pairs={{8,136},{24,152},{40,168},{56,184},{72,200},{88,216},{104,232},{12... | collective-permute-start | bytes 258056 | tf_op jit(solution)/shard_map/ppermute | solution.py:38
  186.9 3.0 collective-permute-start.32
  190.0 3.7 %copy-done.2 = bf16[1,768,6144]{2,1,0:T(8,128)(2,1)S(1)} copy-done((bf16[1,768,6144]{2,1,0:T(8,128)(2,1)S(1)}, bf16[1,768,6144]{2,1,0:T(8,128)(2,1)}, u32[]{:S(2)}) %copy-start.2) | copy-done | bytes 9437208
  193.7 6.9 %shard_map.82 = (bf16[4,144,768]{2,1,0:T(8,128)(2,1)}, bf16[4,144,768]{2,1,0:T(8,128)(2,1)S(1)}, bf16[2,144,768]{2,1,0:T(8,128)(2,1)S(1)}, bf16[2,144,768]{2,1,0:T(8,128)(2,1)S(1)}, bf16[4,144,768]{2,1,0:T(8,128)(2,1)S(1)}) custom-call(s32[8]{0:T(128)S(1)} %stack.32.ids_ref, bf16[288,768]{1,0:T(8,128)(2,1)S(1)} %fusion.5.x_ref, bf16[768,6144]{1,0:T(8,128)(2,1)S(1)} %bitcast.57), custom_call_target="tpu_custom_call" | custom-call | flops 2717908992 | bytes 12976128 | tf_op jit(solution)/shard_map/pallas_call | solution.py:61
  200.6 1.9 collective-permute-start.31
  202.6 2.9 collective-permute-start.30
  205.5 3.1 collective-permute-start.25
  208.9 1.3 shard_map.85
  215.9 3.4 collective-permute-start.24
  223.2 4.7 %collective-permute-start.37 = (bf16[21,16,128]{2,1,0:T(8,128)(2,1)S(1)}, bf16[21,16,128]{2,1,0:T(8,128)(2,1)S(1)}, u32[]{:S(2)}, u32[]{:S(2)}) collective-permute-start(bf16[21,16,128]{2,1,0:T(8,128)(2,1)S(1)} %add_convert_fusion.13.near_ref), channel_id=1, source_target_pairs={{8,24},{24,8},{40,56},{56,40},{72,88},{88,72},{104,120},{120,104},... | collective-permute-start | bytes 258056 | tf_op jit(solution)/shard_map/ppermute | solution.py:38
  228.1 1.9 collective-permute-done.37.far_ref
  231.2 2.5 collective-permute-done.22
  233.6 7.7 %collective-permute-start.38 = (bf16[3,16,128]{2,1,0:T(8,128)(2,1)S(1)}, bf16[3,16,128]{2,1,0:T(8,128)(2,1)S(1)}, u32[]{:S(2)}, u32[]{:S(2)}) collective-permute-start(bf16[3,16,128]{2,1,0:T(8,128)(2,1)S(1)} %get-tuple-element.83), channel_id=1, source_target_pairs={{8,0},{24,16},{40,32},{56,48},{72,64},{88,80},{104,96},{120,112},{... | collective-permute-start | bytes 36872 | tf_op jit(solution)/shard_map/ppermute | solution.py:38
  241.4 2.6 collective-permute-start.39
  244.6 2.8 collective-permute-start.40
  247.4 1.6 collective-permute-start.41
  250.1 2.3 collective-permute-start.42
  252.5 1.9 collective-permute-start.43
  254.4 9.5 %collective-permute-start.44 = (bf16[3,16,128]{2,1,0:T(8,128)(2,1)S(1)}, bf16[3,16,128]{2,1,0:T(8,128)(2,1)S(1)}, u32[]{:S(2)}, u32[]{:S(2)}) collective-permute-start(bf16[3,16,128]{2,1,0:T(8,128)(2,1)S(1)} %get-tuple-element.89), channel_id=1, source_target_pairs={{8,192},{24,208},{40,224},{56,240},{72,0},{88,16},{104,32},{120,48... | collective-permute-start | bytes 36872 | tf_op jit(solution)/shard_map/ppermute | solution.py:38
  263.9 12.9 %collective-permute-start.45 = (bf16[3,16,128]{2,1,0:T(8,128)(2,1)S(1)}, bf16[3,16,128]{2,1,0:T(8,128)(2,1)S(1)}, u32[]{:S(2)}, u32[]{:S(2)}) collective-permute-start(bf16[3,16,128]{2,1,0:T(8,128)(2,1)S(1)} %get-tuple-element.90), channel_id=1, source_target_pairs={{8,224},{24,240},{40,0},{56,16},{72,32},{88,48},{104,64},{120,80},... | collective-permute-start | bytes 36872 | tf_op jit(solution)/shard_map/ppermute | solution.py:38
  280.8 3.3 collective-permute-start.26
  284.2 3.2 collective-permute-start.27
  291.4 3.7 %copy-done.3 = bf16[1,768,6144]{2,1,0:T(8,128)(2,1)S(1)} copy-done((bf16[1,768,6144]{2,1,0:T(8,128)(2,1)S(1)}, bf16[1,768,6144]{2,1,0:T(8,128)(2,1)}, u32[]{:S(2)}) %copy-start.3) | copy-done | bytes 9437208
  295.0 2.9 shard_map.81
  301.1 3.1 collective-permute-start.14
  304.2 4.3 %collective-permute-done.60.rest_14_ = bf16[3,16,128]{2,1,0:T(8,128)(2,1)S(1)} collective-permute-done((bf16[3,16,128]{2,1,0:T(8,128)(2,1)S(1)}, bf16[3,16,128]{2,1,0:T(8,128)(2,1)S(1)}, u32[]{:S(2)}, u32[]{:S(2)}) %collective-permute-start.60) | collective-permute-done | bytes 12320 | tf_op jit(solution)/shard_map/ppermute | solution.py:38
  310.8 3.7 %copy-done.4 = bf16[1,768,6144]{2,1,0:T(8,128)(2,1)S(1)} copy-done((bf16[1,768,6144]{2,1,0:T(8,128)(2,1)S(1)}, bf16[1,768,6144]{2,1,0:T(8,128)(2,1)}, u32[]{:S(2)}) %copy-start.4) | copy-done | bytes 9437208
  314.5 2.9 shard_map.80
  317.4 1.4 convert_add_fusion.3
  320.3 1.9 collective-permute-start.16
  322.2 4.7 %collective-permute-start.15 = (bf16[2,112,768]{2,1,0:T(8,128)(2,1)S(1)}, bf16[2,112,768]{2,1,0:T(8,128)(2,1)S(1)}, u32[]{:S(2)}, u32[]{:S(2)}) collective-permute-start(bf16[2,112,768]{2,1,0:T(8,128)(2,1)S(1)} %get-tuple-element.116), channel_id=1, source_target_pairs={{8,11},{9,8},{10,9},{11,10},{12,15},{13,12},{14,13},{15,14},{24,27... | collective-permute-start | bytes 1032200 | tf_op jit(solution)/shard_map/ppermute | solution.py:21
  327.0 3.2 collective-permute-start.28
  331.2 2.3 collective-permute-start.17
  333.6 4.6 %collective-permute-start.18 = (bf16[1,112,768]{2,1,0:T(8,128)(2,1)S(1)}, bf16[1,112,768]{2,1,0:T(8,128)(2,1)S(1)}, u32[]{:S(2)}, u32[]{:S(2)}) collective-permute-start(bf16[1,112,768]{2,1,0:T(8,128)(2,1)S(1)} %get-tuple-element.114), channel_id=1, source_target_pairs={{8,11},{9,8},{10,9},{11,10},{12,15},{13,12},{14,13},{15,14},{24,27... | collective-permute-start | bytes 516104 | tf_op jit(solution)/shard_map/ppermute | solution.py:21
  339.0 1.5 collective-permute-done.18
  (183 shorter events, 48.1 us)
Async XLA Ops:
  12.3 68.4 %collective-permute-start.9 = (bf16[4,144,768]{2,1,0:T(8,128)(2,1)S(1)}, bf16[4,144,768]{2,1,0:T(8,128)(2,1)S(1)}, u32[]{:S(2)}, u32[]{:S(2)}) collective-permute-start(bf16[4,144,768]{2,1,0:T(8,128)(2,1)S(1)} %get-tuple-element.63), channel_id=1, source_target_pairs={{0,1},{1,2},{2,3},{3,0},{4,5},{5,6},{6,7},{7,4},{16,17},{17,18},{1... | collective-permute-start | bytes 2654216 | tf_op jit(solution)/shard_map/ppermute | solution.py:21
  13.1 68.5 %collective-permute-start.8 = (bf16[4,144,768]{2,1,0:T(8,128)(2,1)S(1)}, bf16[4,144,768]{2,1,0:T(8,128)(2,1)S(1)}, u32[]{:S(2)}, u32[]{:S(2)}) collective-permute-start(bf16[4,144,768]{2,1,0:T(8,128)(2,1)S(1)} %get-tuple-element.61), channel_id=1, source_target_pairs={{0,3},{1,0},{2,1},{3,2},{4,7},{5,4},{6,5},{7,6},{16,19},{17,16},{1... | collective-permute-start | bytes 2654216 | tf_op jit(solution)/shard_map/ppermute | solution.py:21
  14.0 36.4 %collective-permute-start.5 = (f32[4,128]{1,0:T(4,128)S(1)}, f32[4,128]{1,0:T(4,128)S(1)}, u32[]{:S(2)}, u32[]{:S(2)}) collective-permute-start(f32[4,128]{1,0:T(4,128)S(1)} %multiply_reduce_fusion), channel_id=1, source_target_pairs={{0,4},{1,5},{2,6},{3,7},{4,0},{5,1},{6,2},{7,3},{8,12},{9,13},{10,... | collective-permute-start | bytes 6152 | tf_op jit(solution)/shard_map/ppermute | solution.py:21
  35.3 47.6 %collective-permute-start = (bf16[8,112,768]{2,1,0:T(8,128)(2,1)S(1)}, bf16[8,112,768]{2,1,0:T(8,128)(2,1)S(1)}, u32[]{:S(2)}, u32[]{:S(2)}) collective-permute-start(bf16[8,112,768]{2,1,0:T(8,128)(2,1)S(1)} %shard_map.78), channel_id=1, source_target_pairs={{0,4},{1,5},{2,6},{3,7},{4,0},{5,1},{6,2},{7,3},{16,20},{17,21},{1... | collective-permute-start | bytes 4128776 | tf_op jit(solution)/shard_map/ppermute | solution.py:21
  36.1 53.8 %collective-permute-start.29 = (f32[772]{0:T(1024)S(1)}, f32[772]{0:T(1024)S(1)}, u32[]{:S(2)}, u32[]{:S(2)}) collective-permute-start(f32[772]{0:T(1024)S(1)} %pad_maximum_fusion.3), channel_id=1, source_target_pairs={{0,8},{8,0},{1,9},{9,1},{2,10},{10,2},{3,11},{11,3},{4,12},{12,4},... | collective-permute-start | bytes 9272 | tf_op jit(solution)/shard_map/ppermute | solution.py:277
  50.5 14.2 %collective-permute-start.6 = (f32[4,128]{1,0:T(4,128)S(1)}, f32[4,128]{1,0:T(4,128)S(1)}, u32[]{:S(2)}, u32[]{:S(2)}) collective-permute-start(f32[4,128]{1,0:T(4,128)S(1)} %add.314), channel_id=1, source_target_pairs={{0,1},{1,0},{2,3},{3,2},{4,5},{5,4},{6,7},{7,6},{8,9},{9,8},{10,11... | collective-permute-start | bytes 6152 | tf_op jit(solution)/shard_map/ppermute | solution.py:21
  64.7 16.1 %collective-permute-start.7 = (f32[4,128]{1,0:T(4,128)S(1)}, f32[4,128]{1,0:T(4,128)S(1)}, u32[]{:S(2)}, u32[]{:S(2)}) collective-permute-start(f32[4,128]{1,0:T(4,128)S(1)} %add.315), channel_id=1, source_target_pairs={{0,2},{1,3},{2,0},{3,1},{4,6},{5,7},{6,4},{7,5},{8,10},{9,11},{10,... | collective-permute-start | bytes 6152 | tf_op jit(solution)/shard_map/ppermute | solution.py:21
  90.0 96.9 %collective-permute-start.23 = (bf16[288,768]{1,0:T(8,128)(2,1)S(1)}, bf16[288,768]{1,0:T(8,128)(2,1)S(1)}, u32[]{:S(2)}, u32[]{:S(2)}) collective-permute-start(bf16[288,768]{1,0:T(8,128)(2,1)S(1)} %fusion.4), channel_id=1, source_target_pairs={{0,8},{1,9},{2,10},{3,11},{4,12},{5,13},{6,14},{7,15},{16,24},{17,... | collective-permute-start | bytes 1327112 | tf_op jit(solution)/shard_map/ppermute | solution.py:33
  93.7 106.9 %collective-permute-start.36 = (bf16[21,16,128]{2,1,0:T(8,128)(2,1)S(1)}, bf16[21,16,128]{2,1,0:T(8,128)(2,1)S(1)}, u32[]{:S(2)}, u32[]{:S(2)}) collective-permute-start(bf16[21,16,128]{2,1,0:T(8,128)(2,1)S(1)} %get-tuple-element.82), channel_id=1, source_target_pairs={{8,232},{24,248},{40,8},{56,24},{72,40},{88,56},{104,72},{120,88},... | collective-permute-start | bytes 258056 | tf_op jit(solution)/shard_map/ppermute | solution.py:38
  153.0 49.6 %collective-permute-start.35 = (bf16[21,16,128]{2,1,0:T(8,128)(2,1)S(1)}, bf16[21,16,128]{2,1,0:T(8,128)(2,1)S(1)}, u32[]{:S(2)}, u32[]{:S(2)}) collective-permute-start(bf16[21,16,128]{2,1,0:T(8,128)(2,1)S(1)} %get-tuple-element.81), channel_id=1, source_target_pairs={{8,200},{24,216},{40,232},{56,248},{72,8},{88,24},{104,40},{120,56... | collective-permute-start | bytes 258056 | tf_op jit(solution)/shard_map/ppermute | solution.py:38
  165.9 39.6 %collective-permute-start.34 = (bf16[21,16,128]{2,1,0:T(8,128)(2,1)S(1)}, bf16[21,16,128]{2,1,0:T(8,128)(2,1)S(1)}, u32[]{:S(2)}, u32[]{:S(2)}) collective-permute-start(bf16[21,16,128]{2,1,0:T(8,128)(2,1)S(1)} %get-tuple-element.80), channel_id=1, source_target_pairs={{8,168},{24,184},{40,200},{56,216},{72,232},{88,248},{104,8},{120,... | collective-permute-start | bytes 258056 | tf_op jit(solution)/shard_map/ppermute | solution.py:38
  178.8 31.5 %collective-permute-start.33 = (bf16[21,16,128]{2,1,0:T(8,128)(2,1)}, bf16[21,16,128]{2,1,0:T(8,128)(2,1)}, u32[]{:S(2)}, u32[]{:S(2)}) collective-permute-start(bf16[21,16,128]{2,1,0:T(8,128)(2,1)} %get-tuple-element.79), channel_id=1, source_target_pairs={{8,136},{24,152},{40,168},{56,184},{72,200},{88,216},{104,232},{12... | collective-permute-start | bytes 258056 | tf_op jit(solution)/shard_map/ppermute | solution.py:38
  186.9 24.0 %collective-permute-start.32 = (bf16[21,16,128]{2,1,0:T(8,128)(2,1)}, bf16[21,16,128]{2,1,0:T(8,128)(2,1)}, u32[]{:S(2)}, u32[]{:S(2)}) collective-permute-start(bf16[21,16,128]{2,1,0:T(8,128)(2,1)} %get-tuple-element.78), channel_id=1, source_target_pairs={{8,104},{24,120},{40,136},{56,152},{72,168},{88,184},{104,200},{12... | collective-permute-start | bytes 258056 | tf_op jit(solution)/shard_map/ppermute | solution.py:38
  200.6 10.9 %collective-permute-start.31 = (bf16[21,16,128]{2,1,0:T(8,128)(2,1)}, bf16[21,16,128]{2,1,0:T(8,128)(2,1)}, u32[]{:S(2)}, u32[]{:S(2)}) collective-permute-start(bf16[21,16,128]{2,1,0:T(8,128)(2,1)} %get-tuple-element.77), channel_id=1, source_target_pairs={{8,72},{24,88},{40,104},{56,120},{72,136},{88,152},{104,168},{120,... | collective-permute-start | bytes 258056 | tf_op jit(solution)/shard_map/ppermute | solution.py:38
  202.6 9.9 %collective-permute-start.30 = (bf16[21,16,128]{2,1,0:T(8,128)(2,1)}, bf16[21,16,128]{2,1,0:T(8,128)(2,1)}, u32[]{:S(2)}, u32[]{:S(2)}) collective-permute-start(bf16[21,16,128]{2,1,0:T(8,128)(2,1)} %get-tuple-element.76), channel_id=1, source_target_pairs={{8,40},{24,56},{40,72},{56,88},{72,104},{88,120},{104,136},{120,15... | collective-permute-start | bytes 258056 | tf_op jit(solution)/shard_map/ppermute | solution.py:38
  205.5 41.9 %collective-permute-start.25 = (bf16[4,144,768]{2,1,0:T(8,128)(2,1)}, bf16[4,144,768]{2,1,0:T(8,128)(2,1)}, u32[]{:S(2)}, u32[]{:S(2)}) collective-permute-start(bf16[4,144,768]{2,1,0:T(8,128)(2,1)} %get-tuple-element.73), channel_id=1, source_target_pairs={{8,9},{9,10},{10,11},{11,8},{12,13},{13,14},{14,15},{15,12},{24,25... | collective-permute-start | bytes 2654216 | tf_op jit(solution)/shard_map/ppermute | solution.py:21
  213.9 6.7 %collective-permute-start.48 = (bf16[21,16,128]{2,1,0:T(8,128)(2,1)S(1)}, bf16[21,16,128]{2,1,0:T(8,128)(2,1)S(1)}, u32[]{:S(2)}, u32[]{:S(2)}) collective-permute-start(bf16[21,16,128]{2,1,0:T(8,128)(2,1)S(1)} %get-tuple-element.94), channel_id=1, source_target_pairs={{0,96},{16,112},{32,128},{48,144},{64,160},{80,176},{96,192},{112,... | collective-permute-start | bytes 258056 | tf_op jit(solution)/shard_map/ppermute | solution.py:38
  214.6 7.3 %collective-permute-start.47 = (bf16[21,16,128]{2,1,0:T(8,128)(2,1)S(1)}, bf16[21,16,128]{2,1,0:T(8,128)(2,1)S(1)}, u32[]{:S(2)}, u32[]{:S(2)}) collective-permute-start(bf16[21,16,128]{2,1,0:T(8,128)(2,1)S(1)} %get-tuple-element.93), channel_id=1, source_target_pairs={{0,64},{16,80},{32,96},{48,112},{64,128},{80,144},{96,160},{112,17... | collective-permute-start | bytes 258056 | tf_op jit(solution)/shard_map/ppermute | solution.py:38
  215.2 7.9 %collective-permute-start.46 = (bf16[21,16,128]{2,1,0:T(8,128)(2,1)S(1)}, bf16[21,16,128]{2,1,0:T(8,128)(2,1)S(1)}, u32[]{:S(2)}, u32[]{:S(2)}) collective-permute-start(bf16[21,16,128]{2,1,0:T(8,128)(2,1)S(1)} %get-tuple-element.92), channel_id=1, source_target_pairs={{0,32},{16,48},{32,64},{48,80},{64,96},{80,112},{96,128},{112,144}... | collective-permute-start | bytes 258056 | tf_op jit(solution)/shard_map/ppermute | solution.py:38
  215.9 48.0 %collective-permute-start.24 = (bf16[4,144,768]{2,1,0:T(8,128)(2,1)S(1)}, bf16[4,144,768]{2,1,0:T(8,128)(2,1)S(1)}, u32[]{:S(2)}, u32[]{:S(2)}) collective-permute-start(bf16[4,144,768]{2,1,0:T(8,128)(2,1)S(1)} %get-tuple-element.71), channel_id=1, source_target_pairs={{8,11},{9,8},{10,9},{11,10},{12,15},{13,12},{14,13},{15,14},{24,27... | collective-permute-start | bytes 2654216 | tf_op jit(solution)/shard_map/ppermute | solution.py:21
  220.6 63.6 %collective-permute-start.13 = (bf16[224,768]{1,0:T(8,128)(2,1)S(1)}, bf16[224,768]{1,0:T(8,128)(2,1)S(1)}, u32[]{:S(2)}, u32[]{:S(2)}) collective-permute-start(bf16[224,768]{1,0:T(8,128)(2,1)S(1)} %copy-done.10), channel_id=1, source_target_pairs={{0,8},{1,9},{2,10},{3,11},{4,12},{5,13},{6,14},{7,15},{16,24},{17,... | collective-permute-start | bytes 1032200 | tf_op jit(solution)/shard_map/ppermute | solution.py:33
  221.9 11.7 %collective-permute-start.22 = (f32[4,128]{1,0:T(4,128)S(1)}, f32[4,128]{1,0:T(4,128)S(1)}, u32[]{:S(2)}, u32[]{:S(2)}) collective-permute-start(f32[4,128]{1,0:T(4,128)S(1)} %get-tuple-element.108), channel_id=1, source_target_pairs={{0,8},{1,9},{2,10},{3,11},{4,12},{5,13},{6,14},{7,15},{16,24},{17,... | collective-permute-start | bytes 6152 | tf_op jit(solution)/shard_map/ppermute | solution.py:33
  223.2 6.7 %collective-permute-start.37 = (bf16[21,16,128]{2,1,0:T(8,128)(2,1)S(1)}, bf16[21,16,128]{2,1,0:T(8,128)(2,1)S(1)}, u32[]{:S(2)}, u32[]{:S(2)}) collective-permute-start(bf16[21,16,128]{2,1,0:T(8,128)(2,1)S(1)} %add_convert_fusion.13.near_ref), channel_id=1, source_target_pairs={{8,24},{24,8},{40,56},{56,40},{72,88},{88,72},{104,120},{120,104},... | collective-permute-start | bytes 258056 | tf_op jit(solution)/shard_map/ppermute | solution.py:38
  229.9 11.5 %collective-permute-start.53 = (bf16[21,16,128]{2,1,0:T(8,128)(2,1)S(1)}, bf16[21,16,128]{2,1,0:T(8,128)(2,1)S(1)}, u32[]{:S(2)}, u32[]{:S(2)}) collective-permute-start(bf16[21,16,128]{2,1,0:T(8,128)(2,1)S(1)} %add_convert_fusion.12.near_ref), channel_id=1, source_target_pairs={{0,16},{16,0},{32,48},{48,32},{64,80},{80,64},{96,112},{112,96},{1... | collective-permute-start | bytes 258056 | tf_op jit(solution)/shard_map/ppermute | solution.py:38
  233.6 11.0 %collective-permute-start.38 = (bf16[3,16,128]{2,1,0:T(8,128)(2,1)S(1)}, bf16[3,16,128]{2,1,0:T(8,128)(2,1)S(1)}, u32[]{:S(2)}, u32[]{:S(2)}) collective-permute-start(bf16[3,16,128]{2,1,0:T(8,128)(2,1)S(1)} %get-tuple-element.83), channel_id=1, source_target_pairs={{8,0},{24,16},{40,32},{56,48},{72,64},{88,80},{104,96},{120,112},{... | collective-permute-start | bytes 36872 | tf_op jit(solution)/shard_map/ppermute | solution.py:38
  241.4 8.7 %collective-permute-start.39 = (bf16[3,16,128]{2,1,0:T(8,128)(2,1)S(1)}, bf16[3,16,128]{2,1,0:T(8,128)(2,1)S(1)}, u32[]{:S(2)}, u32[]{:S(2)}) collective-permute-start(bf16[3,16,128]{2,1,0:T(8,128)(2,1)S(1)} %get-tuple-element.84), channel_id=1, source_target_pairs={{8,32},{24,48},{40,64},{56,80},{72,96},{88,112},{104,128},{120,144... | collective-permute-start | bytes 36872 | tf_op jit(solution)/shard_map/ppermute | solution.py:38
  244.6 7.8 %collective-permute-start.40 = (bf16[3,16,128]{2,1,0:T(8,128)(2,1)S(1)}, bf16[3,16,128]{2,1,0:T(8,128)(2,1)S(1)}, u32[]{:S(2)}, u32[]{:S(2)}) collective-permute-start(bf16[3,16,128]{2,1,0:T(8,128)(2,1)S(1)} %get-tuple-element.85), channel_id=1, source_target_pairs={{8,64},{24,80},{40,96},{56,112},{72,128},{88,144},{104,160},{120,1... | collective-permute-start | bytes 36872 | tf_op jit(solution)/shard_map/ppermute | solution.py:38
  247.4 6.9 %collective-permute-start.41 = (bf16[3,16,128]{2,1,0:T(8,128)(2,1)S(1)}, bf16[3,16,128]{2,1,0:T(8,128)(2,1)S(1)}, u32[]{:S(2)}, u32[]{:S(2)}) collective-permute-start(bf16[3,16,128]{2,1,0:T(8,128)(2,1)S(1)} %get-tuple-element.86), channel_id=1, source_target_pairs={{8,96},{24,112},{40,128},{56,144},{72,160},{88,176},{104,192},{120... | collective-permute-start | bytes 36872 | tf_op jit(solution)/shard_map/ppermute | solution.py:38
  250.1 26.8 %collective-permute-start.42 = (bf16[3,16,128]{2,1,0:T(8,128)(2,1)S(1)}, bf16[3,16,128]{2,1,0:T(8,128)(2,1)S(1)}, u32[]{:S(2)}, u32[]{:S(2)}) collective-permute-start(bf16[3,16,128]{2,1,0:T(8,128)(2,1)S(1)} %get-tuple-element.87), channel_id=1, source_target_pairs={{8,128},{24,144},{40,160},{56,176},{72,192},{88,208},{104,224},{12... | collective-permute-start | bytes 36872 | tf_op jit(solution)/shard_map/ppermute | solution.py:38
  252.5 25.7 %collective-permute-start.43 = (bf16[3,16,128]{2,1,0:T(8,128)(2,1)S(1)}, bf16[3,16,128]{2,1,0:T(8,128)(2,1)S(1)}, u32[]{:S(2)}, u32[]{:S(2)}) collective-permute-start(bf16[3,16,128]{2,1,0:T(8,128)(2,1)S(1)} %get-tuple-element.88), channel_id=1, source_target_pairs={{8,160},{24,176},{40,192},{56,208},{72,224},{88,240},{104,0},{120,... | collective-permute-start | bytes 36872 | tf_op jit(solution)/shard_map/ppermute | solution.py:38
  254.4 25.2 %collective-permute-start.44 = (bf16[3,16,128]{2,1,0:T(8,128)(2,1)S(1)}, bf16[3,16,128]{2,1,0:T(8,128)(2,1)S(1)}, u32[]{:S(2)}, u32[]{:S(2)}) collective-permute-start(bf16[3,16,128]{2,1,0:T(8,128)(2,1)S(1)} %get-tuple-element.89), channel_id=1, source_target_pairs={{8,192},{24,208},{40,224},{56,240},{72,0},{88,16},{104,32},{120,48... | collective-permute-start | bytes 36872 | tf_op jit(solution)/shard_map/ppermute | solution.py:38
  263.9 16.9 %collective-permute-start.45 = (bf16[3,16,128]{2,1,0:T(8,128)(2,1)S(1)}, bf16[3,16,128]{2,1,0:T(8,128)(2,1)S(1)}, u32[]{:S(2)}, u32[]{:S(2)}) collective-permute-start(bf16[3,16,128]{2,1,0:T(8,128)(2,1)S(1)} %get-tuple-element.90), channel_id=1, source_target_pairs={{8,224},{24,240},{40,0},{56,16},{72,32},{88,48},{104,64},{120,80},... | collective-permute-start | bytes 36872 | tf_op jit(solution)/shard_map/ppermute | solution.py:38
  276.9 10.5 %collective-permute-start.54 = (bf16[3,16,128]{2,1,0:T(8,128)(2,1)S(1)}, bf16[3,16,128]{2,1,0:T(8,128)(2,1)S(1)}, u32[]{:S(2)}, u32[]{:S(2)}) collective-permute-start(bf16[3,16,128]{2,1,0:T(8,128)(2,1)S(1)} %get-tuple-element.99), channel_id=1, source_target_pairs={{0,8},{16,24},{32,40},{48,56},{64,72},{80,88},{96,104},{112,120},{... | collective-permute-start | bytes 36872 | tf_op jit(solution)/shard_map/ppermute | solution.py:38
  278.2 10.5 %collective-permute-start.55 = (bf16[3,16,128]{2,1,0:T(8,128)(2,1)S(1)}, bf16[3,16,128]{2,1,0:T(8,128)(2,1)S(1)}, u32[]{:S(2)}, u32[]{:S(2)}) collective-permute-start(bf16[3,16,128]{2,1,0:T(8,128)(2,1)S(1)} %get-tuple-element.100), channel_id=1, source_target_pairs={{0,40},{16,56},{32,72},{48,88},{64,104},{80,120},{96,136},{112,152... | collective-permute-start | bytes 36872 | tf_op jit(solution)/shard_map/ppermute | solution.py:38
  279.5 10.5 %collective-permute-start.56 = (bf16[3,16,128]{2,1,0:T(8,128)(2,1)S(1)}, bf16[3,16,128]{2,1,0:T(8,128)(2,1)S(1)}, u32[]{:S(2)}, u32[]{:S(2)}) collective-permute-start(bf16[3,16,128]{2,1,0:T(8,128)(2,1)S(1)} %get-tuple-element.101), channel_id=1, source_target_pairs={{0,72},{16,88},{32,104},{48,120},{64,136},{80,152},{96,168},{112,1... | collective-permute-start | bytes 36872 | tf_op jit(solution)/shard_map/ppermute | solution.py:38
  280.8 36.5 %collective-permute-start.26 = (bf16[2,144,768]{2,1,0:T(8,128)(2,1)S(1)}, bf16[2,144,768]{2,1,0:T(8,128)(2,1)S(1)}, u32[]{:S(2)}, u32[]{:S(2)}) collective-permute-start(bf16[2,144,768]{2,1,0:T(8,128)(2,1)S(1)} %add_convert_fusion.1), channel_id=1, source_target_pairs={{8,9},{9,10},{10,11},{11,8},{12,13},{13,14},{14,15},{15,12},{24,25... | collective-permute-start | bytes 1327112 | tf_op jit(solution)/shard_map/ppermute | solution.py:21
  284.2 33.2 %collective-permute-start.27 = (bf16[2,144,768]{2,1,0:T(8,128)(2,1)S(1)}, bf16[2,144,768]{2,1,0:T(8,128)(2,1)S(1)}, u32[]{:S(2)}, u32[]{:S(2)}) collective-permute-start(bf16[2,144,768]{2,1,0:T(8,128)(2,1)S(1)} %add_convert_fusion), channel_id=1, source_target_pairs={{8,11},{9,8},{10,9},{11,10},{12,15},{13,12},{14,13},{15,14},{24,27... | collective-permute-start | bytes 1327112 | tf_op jit(solution)/shard_map/ppermute | solution.py:21
  287.4 10.5 %collective-permute-start.57 = (bf16[3,16,128]{2,1,0:T(8,128)(2,1)S(1)}, bf16[3,16,128]{2,1,0:T(8,128)(2,1)S(1)}, u32[]{:S(2)}, u32[]{:S(2)}) collective-permute-start(bf16[3,16,128]{2,1,0:T(8,128)(2,1)S(1)} %get-tuple-element.102), channel_id=1, source_target_pairs={{0,104},{16,120},{32,136},{48,152},{64,168},{80,184},{96,200},{112... | collective-permute-start | bytes 36872 | tf_op jit(solution)/shard_map/ppermute | solution.py:38
  288.8 10.9 %collective-permute-start.58 = (bf16[3,16,128]{2,1,0:T(8,128)(2,1)S(1)}, bf16[3,16,128]{2,1,0:T(8,128)(2,1)S(1)}, u32[]{:S(2)}, u32[]{:S(2)}) collective-permute-start(bf16[3,16,128]{2,1,0:T(8,128)(2,1)S(1)} %get-tuple-element.103), channel_id=1, source_target_pairs={{0,136},{16,152},{32,168},{48,184},{64,200},{80,216},{96,232},{112... | collective-permute-start | bytes 36872 | tf_op jit(solution)/shard_map/ppermute | solution.py:38
  290.1 11.0 %collective-permute-start.59 = (bf16[3,16,128]{2,1,0:T(8,128)(2,1)S(1)}, bf16[3,16,128]{2,1,0:T(8,128)(2,1)S(1)}, u32[]{:S(2)}, u32[]{:S(2)}) collective-permute-start(bf16[3,16,128]{2,1,0:T(8,128)(2,1)S(1)} %get-tuple-element.104), channel_id=1, source_target_pairs={{0,168},{16,184},{32,200},{48,216},{64,232},{80,248},{96,8},{112,2... | collective-permute-start | bytes 36872 | tf_op jit(solution)/shard_map/ppermute | solution.py:38
  297.9 10.6 %collective-permute-start.60 = (bf16[3,16,128]{2,1,0:T(8,128)(2,1)S(1)}, bf16[3,16,128]{2,1,0:T(8,128)(2,1)S(1)}, u32[]{:S(2)}, u32[]{:S(2)}) collective-permute-start(bf16[3,16,128]{2,1,0:T(8,128)(2,1)S(1)} %get-tuple-element.105), channel_id=1, source_target_pairs={{0,200},{16,216},{32,232},{48,248},{64,8},{80,24},{96,40},{112,56}... | collective-permute-start | bytes 36872 | tf_op jit(solution)/shard_map/ppermute | solution.py:38
  299.6 9.9 %collective-permute-start.61 = (bf16[3,16,128]{2,1,0:T(8,128)(2,1)S(1)}, bf16[3,16,128]{2,1,0:T(8,128)(2,1)S(1)}, u32[]{:S(2)}, u32[]{:S(2)}) collective-permute-start(bf16[3,16,128]{2,1,0:T(8,128)(2,1)S(1)} %get-tuple-element.106), channel_id=1, source_target_pairs={{0,232},{16,248},{32,8},{48,24},{64,40},{80,56},{96,72},{112,88},{... | collective-permute-start | bytes 36872 | tf_op jit(solution)/shard_map/ppermute | solution.py:38
  301.1 19.0 %collective-permute-start.14 = (bf16[8,112,768]{2,1,0:T(8,128)(2,1)S(1)}, bf16[8,112,768]{2,1,0:T(8,128)(2,1)S(1)}, u32[]{:S(2)}, u32[]{:S(2)}) collective-permute-start(bf16[8,112,768]{2,1,0:T(8,128)(2,1)S(1)} %shard_map.81), channel_id=1, source_target_pairs={{8,12},{9,13},{10,14},{11,15},{12,8},{13,9},{14,10},{15,11},{24,28... | collective-permute-start | bytes 4128776 | tf_op jit(solution)/shard_map/ppermute | solution.py:21
  320.3 9.9 %collective-permute-start.16 = (bf16[2,112,768]{2,1,0:T(8,128)(2,1)S(1)}, bf16[2,112,768]{2,1,0:T(8,128)(2,1)S(1)}, u32[]{:S(2)}, u32[]{:S(2)}) collective-permute-start(bf16[2,112,768]{2,1,0:T(8,128)(2,1)S(1)} %get-tuple-element.115), channel_id=1, source_target_pairs={{8,9},{9,10},{10,11},{11,8},{12,13},{13,14},{14,15},{15,12},{24,25... | collective-permute-start | bytes 1032200 | tf_op jit(solution)/shard_map/ppermute | solution.py:21
  322.2 8.9 %collective-permute-start.15 = (bf16[2,112,768]{2,1,0:T(8,128)(2,1)S(1)}, bf16[2,112,768]{2,1,0:T(8,128)(2,1)S(1)}, u32[]{:S(2)}, u32[]{:S(2)}) collective-permute-start(bf16[2,112,768]{2,1,0:T(8,128)(2,1)S(1)} %get-tuple-element.116), channel_id=1, source_target_pairs={{8,11},{9,8},{10,9},{11,10},{12,15},{13,12},{14,13},{15,14},{24,27... | collective-permute-start | bytes 1032200 | tf_op jit(solution)/shard_map/ppermute | solution.py:21
  327.0 11.2 %collective-permute-start.28 = (bf16[288,768]{1,0:T(8,128)(2,1)S(1)}, bf16[288,768]{1,0:T(8,128)(2,1)S(1)}, u32[]{:S(2)}, u32[]{:S(2)}) collective-permute-start(bf16[288,768]{1,0:T(8,128)(2,1)S(1)} %pad_maximum_fusion.2), channel_id=1, source_target_pairs={{8,12},{9,13},{10,14},{11,15},{12,8},{13,9},{14,10},{15,11},{24,28... | collective-permute-start | bytes 1327112 | tf_op jit(solution)/shard_map/ppermute | solution.py:21
  331.2 7.8 %collective-permute-start.17 = (bf16[1,112,768]{2,1,0:T(8,128)(2,1)S(1)}, bf16[1,112,768]{2,1,0:T(8,128)(2,1)S(1)}, u32[]{:S(2)}, u32[]{:S(2)}) collective-permute-start(bf16[1,112,768]{2,1,0:T(8,128)(2,1)S(1)} %get-tuple-element.113), channel_id=1, source_target_pairs={{8,9},{9,10},{10,11},{11,8},{12,13},{13,14},{14,15},{15,12},{24,25... | collective-permute-start | bytes 516104 | tf_op jit(solution)/shard_map/ppermute | solution.py:21
  333.6 7.0 %collective-permute-start.18 = (bf16[1,112,768]{2,1,0:T(8,128)(2,1)S(1)}, bf16[1,112,768]{2,1,0:T(8,128)(2,1)S(1)}, u32[]{:S(2)}, u32[]{:S(2)}) collective-permute-start(bf16[1,112,768]{2,1,0:T(8,128)(2,1)S(1)} %get-tuple-element.114), channel_id=1, source_target_pairs={{8,11},{9,8},{10,9},{11,10},{12,15},{13,12},{14,13},{15,14},{24,27... | collective-permute-start | bytes 516104 | tf_op jit(solution)/shard_map/ppermute | solution.py:21
  (32 other events, 152.7 us)
